TPU v7x, 256 devices: a whole 4x4x8 slice. The times are simulated.
256 devices in a mesh: shot: 16 (over y, x_hi, core), slab: 16 (over x_lo, z).
Axes of the slice: x: 4 (x_hi: 2, x_lo: 2; x = x_hi * 2 + x_lo), y: 4, z: 8, core: 2. Of those that a mesh axis runs over, the one named last changes fastest.
Arguments:
- pressure_old: float32 [16, 640, 32, 128], P('shot', 'slab'), may hold values from -6 to 6
- pressure_now: float32 [16, 640, 32, 128], P('shot', 'slab'), may hold values from -6 to 6
- adjoint_later: float32 [16, 640, 32, 128], P('shot', 'slab'), may hold values from -6 to 6
- adjoint_now: float32 [16, 640, 32, 128], P('shot', 'slab'), may hold values from -6 to 6
- stiffness: float32 [640, 32, 128], P('slab'), may hold values from 0.02 to 0.12
- buoyancy: float32 [640, 32, 128], P('slab'), may hold values from 0.5 to 1.5
- traces: float32 [16, 4096, 2048], P('shot', 'slab'), may hold values from -6 to 6
- owner_slab: int32 [16, 4096, 1], P('shot', 'slab'), may hold values from 0 to 15; in each aligned block of 256 rows (0 to 255, 256 to 511, ..., all dimensions but the last counted through in order) at most 32 rows name the same one
- depth_plane: int32 [16, 4096], P('shot', 'slab'), may hold values from 0 to 39
- station_cell: int32 [16, 4096], P('shot', 'slab'), may hold values from 0 to 4095
- resampler: float32 [2, 2048], replicated, may hold values from -3 to 3
Outputs:
- gradient: float32 [640, 32, 128], P('slab', 'shot')
- adjoint_field: float32 [16, 640, 32, 128], P('shot', 'slab')
Inputs may be any that keep to these rules, and one draw needn't show every extreme that they name: `owner_slab`: within each shot, among the 256 rows of each aligned block of rows, at most 32 name the same owner slab, a bound that some block reaches.
All inputs are finite; a program needn't handle non-finite values.
Results may differ from a plain program's by a relative error of at most 0.0003.
Values sent between devices are 32-bit elements; how exact they have to be, the bound alone decides.
A program may use at most 128 MiB of HBM per device.

v0:
```python
import jax
import jax.numpy as jnp
from jax import lax
from jax.sharding import PartitionSpec as P

second_taps = (-205.0 / 72.0, 8.0 / 5.0, -1.0 / 5.0, 8.0 / 315.0, -1.0 / 560.0)
first_taps = (0.0, 4.0 / 5.0, -1.0 / 5.0, 4.0 / 105.0, -1.0 / 280.0)


def with_halo(cells, sides, width):
    for axis, dim in sides:
        count = lax.axis_size(axis)
        ends = count - 1
        head = lax.slice_in_dim(cells, 0, width, axis=dim)
        tail = lax.slice_in_dim(cells, cells.shape[dim] - width, cells.shape[dim], axis=dim)
        cells = jnp.concatenate(
            [
                lax.ppermute(tail, axis, [(i, (i + 1) % count) for i in range(ends)]),
                cells,
                lax.ppermute(head, axis, [((i + 1) % count, i) for i in range(ends)]),
            ],
            axis=dim,
        )
    return cells


def shifted(wavefield, offset, dimension):
    length = wavefield.shape[dimension]
    margin = abs(offset)
    shape_list = list(wavefield.shape)
    shape_list[dimension] = margin
    padding = jnp.zeros(tuple(shape_list), wavefield.dtype)
    if offset > 0:
        portion = lax.slice_in_dim(wavefield, margin, length, axis=dimension)
        return jnp.concatenate([portion, padding], axis=dimension)
    portion = lax.slice_in_dim(wavefield, 0, length - margin, axis=dimension)
    return jnp.concatenate([padding, portion], axis=dimension)


def derivatives(extended, planes):
    center = extended[4 : 4 + planes]
    second = 3.0 * second_taps[0] * center
    slope_depth = jnp.zeros_like(center)
    slope_across = jnp.zeros_like(center)
    slope_along = jnp.zeros_like(center)
    for offset in range(1, 5):
        upward = extended[4 + offset : 4 + offset + planes]
        downward = extended[4 - offset : 4 - offset + planes]
        across_up = shifted(center, offset, 1)
        across_down = shifted(center, -offset, 1)
        along_up = shifted(center, offset, 2)
        along_down = shifted(center, -offset, 2)
        second = second + second_taps[offset] * (
            upward + downward + across_up + across_down + along_up + along_down
        )
        slope_depth = slope_depth + first_taps[offset] * (upward - downward)
        slope_across = slope_across + first_taps[offset] * (across_up - across_down)
        slope_along = slope_along + first_taps[offset] * (along_up - along_down)
    return (second, slope_depth, slope_across, slope_along)


def laplace_like(extended, buoyancy, slopes):
    second, slope_depth, slope_across, slope_along = derivatives(extended, buoyancy.shape[0])
    return (
        buoyancy * second
        + slopes[0] * slope_depth
        + slopes[1] * slope_across
        + slopes[2] * slope_along
    )


def on_device(
    pressure_old,
    pressure_now,
    adjoint_later,
    adjoint_now,
    stiffness,
    buoyancy,
    traces,
    owner_slab,
    depth_plane,
    station_cell,
    resampler,
):
    planes = buoyancy.shape[0]
    across = buoyancy.shape[1]
    along = buoyancy.shape[2]
    old_field = pressure_old[0]
    now_field = pressure_now[0]
    later_field = adjoint_later[0]
    adjoint_field = adjoint_now[0]
    owners = owner_slab[0, :, 0]
    row_count = owners.shape[0]
    slab_count = lax.axis_size("slab")
    capacity = 2 * row_count // slab_count
    member = (owners[:, None] == jnp.arange(slab_count, dtype=jnp.int32)[None, :]).astype(
        jnp.float32
    )
    earlier = (jnp.arange(row_count)[:, None] > jnp.arange(row_count)[None, :]).astype(jnp.float32)
    before = jnp.dot(earlier, member, precision=lax.Precision.HIGHEST)
    slot_index = jnp.sum(before * member, axis=1).astype(jnp.int32)
    target = owners * capacity + slot_index
    cells = depth_plane[0] * (across * along) + station_cell[0]
    cell_buffer = (
        jnp.zeros((slab_count * capacity,), jnp.int32)
        .at[target]
        .set(cells)
        .reshape(slab_count, capacity)
    )
    sources = jnp.dot(traces[0], resampler.T, precision=lax.Precision.HIGHEST)
    value_buffer = (
        jnp.zeros((slab_count * capacity, 2), jnp.float32)
        .at[target]
        .set(sources)
        .reshape(slab_count, capacity, 2)
    )
    arrived, arrived_cells = (
        lax.all_to_all(value_buffer, "slab", split_axis=0, concat_axis=0, tiled=True),
        lax.all_to_all(cell_buffer, "slab", split_axis=0, concat_axis=0, tiled=True),
    )
    flat_cells = arrived_cells.reshape(-1)
    volume = planes * across * along
    inject_first = (
        jnp.zeros((volume,), jnp.float32)
        .at[flat_cells]
        .add(arrived[:, :, 0].reshape(-1))
        .reshape(planes, across, along)
    )
    inject_second = (
        jnp.zeros((volume,), jnp.float32)
        .at[flat_cells]
        .add(arrived[:, :, 1].reshape(-1))
        .reshape(planes, across, along)
    )
    model_ext = with_halo(buoyancy, (("slab", 0),), 4)
    slopes = derivatives(model_ext, planes)[1:]

    def operate(wavefield):
        extended = with_halo(wavefield, (("slab", 0),), 4)
        return laplace_like(extended, buoyancy, slopes)

    forward_one = 2.0 * now_field - old_field + stiffness * operate(now_field)
    forward_two = 2.0 * forward_one - now_field + stiffness * operate(forward_one)
    adjoint_one = (
        2.0 * adjoint_field - later_field + stiffness * (operate(adjoint_field) + inject_first)
    )
    adjoint_zero = (
        2.0 * adjoint_one - adjoint_field + stiffness * (operate(adjoint_one) + inject_second)
    )
    term_first = adjoint_field * (forward_two - 2.0 * forward_one + now_field)
    term_second = adjoint_one * (forward_one - 2.0 * now_field + old_field)
    gradient = lax.psum_scatter(term_first + term_second, "shot", scatter_dimension=1, tiled=True)
    return (gradient, adjoint_zero[None])


def solution(mesh):
    return jax.shard_map(
        on_device,
        mesh=mesh,
        in_specs=(
            P("shot", "slab", None, None),
            P("shot", "slab", None, None),
            P("shot", "slab", None, None),
            P("shot", "slab", None, None),
            P("slab", None, None),
            P("slab", None, None),
            P("shot", "slab", None),
            P("shot", "slab", None),
            P("shot", "slab"),
            P("shot", "slab"),
            P(),
        ),
        out_specs=(P("slab", "shot", None), P("shot", "slab", None, None)),
        check_vma=False,
    )
```

profile of v0, /device:TPU:1, one launch (start us, length us, event | category | flops | bytes accessed | tf_op | source)
XLA Modules:
  0.0 239.3 jit_solution(319520799892113232)
XLA Ops:
  7.2 1.7 fusion.83
  8.9 5.0 %collective-permute-start.3 = (f32[4,32,128]{2,1,0:T(8,128)}, f32[4,32,128]{2,1,0:T(8,128)}, u32[]{:S(2)}, u32[]{:S(2)}) collective-permute-start(f32[4,32,128]{2,1,0:T(8,128)} %get-tuple-element.85), channel_id=1, source_target_pairs={{0,1},{1,2},{2,3},{3,4},{4,5},{5,6},{6,7},{7,8},{8,9},{9,10},{10,1... | collective-permute-start | bytes 196616 | tf_op jit(solution)/shard_map/ppermute | solution.py:18
  13.8 1.3 collective-permute-start.2
  15.1 1.5 slice_bitcast_fusion.2
  16.7 1.3 collective-permute-start
  17.9 5.2 %collective-permute-start.1 = (f32[4,32,128]{2,1,0:T(8,128)}, f32[4,32,128]{2,1,0:T(8,128)}, u32[]{:S(2)}, u32[]{:S(2)}) collective-permute-start(f32[4,32,128]{2,1,0:T(8,128)} %get-tuple-element.100), channel_id=1, source_target_pairs={{0,1},{1,2},{2,3},{3,4},{4,5},{5,6},{6,7},{7,8},{8,9},{9,10},{10,1... | collective-permute-start | bytes 196616 | tf_op jit(solution)/shard_map/ppermute | solution.py:18
  25.5 1.4 scatter_custom_fusion
  27.6 9.0 %all-to-all-start = ((s32[16,1,32]{2,1,0:T(1,128)}), s32[16,1,32]{2,1,0:T(1,128)S(1)}, u32[]{:S(2)}, u32[]{:S(2)}) async-start(s32[16,1,32]{2,1,0:T(1,128)} %all_to_all.9), calls=%async_computation | async-start | bytes 16384 | tf_op jit(solution)/shard_map/all_to_all | solution.py:119
  36.7 1.5 slice_bitcast_fusion.1
  38.2 1.3 collective-permute-start.6
  39.5 3.8 %fusion.75 = (f32[40,32,127]{2,1,0:T(8,128)}, f32[40,32,127]{2,1,0:T(8,128)}, f32[40,32,127]{2,1,0:T(8,128)}, f32[40,32,127]{2,1,0:T(8,128)}) fusion(f32[40,32,128]{2,1,0:T(8,128)} %param.16, f32[40,32,128]{2,1,0:T(8,128)} %bitcast.54), kind=kLoop, calls=%fused_computation.160 | loop fusion | bytes 5201920 | tf_op jit(solution)/shard_map/slice | solution.py:34
  43.3 1.9 fusion.76
  45.2 1.9 fusion.77
  47.1 1.9 fusion.78
  48.9 1.6 fusion.79
  50.5 1.7 fusion.80
  52.2 1.6 fusion.81
  53.8 1.6 fusion.82
  56.5 1.2 fusion.59
  57.8 1.2 fusion.60
  59.0 1.3 fusion.61
  60.3 1.2 fusion.62
  61.5 1.2 fusion.63
  63.9 1.8 fusion
  65.7 1.3 fusion.65
  68.9 8.5 %all-to-all-start.1 = ((f32[16,32,2]{1,2,0:T(2,128)}), f32[16,32,2]{1,2,0:T(2,128)S(1)}, u32[]{:S(2)}, u32[]{:S(2)}) async-start(f32[16,32,2]{1,2,0:T(2,128)} %copy.56), calls=%async_computation.1 | async-start | bytes 32768 | tf_op jit(solution)/shard_map/all_to_all | solution.py:118
  78.7 6.0 %all-to-all-done.1 = f32[16,32,2]{1,2,0:T(2,128)S(1)} async-done(((f32[16,32,2]{1,2,0:T(2,128)}), f32[16,32,2]{1,2,0:T(2,128)S(1)}, u32[]{:S(2)}, u32[]{:S(2)}) %all-to-all-start.1) | async-done | bytes 4128 | tf_op jit(solution)/shard_map/all_to_all | solution.py:118
  85.0 4.5 %scatter_custom_fusion.2 = f32[163840]{0:T(1024)} fusion(s32[512]{0:T(512)S(1)} %bitcast.67, f32[512]{0:T(512)S(1)} %reshape.113, f32[]{:T(128)} %constant.17.clone.1), kind=kCustom, calls=%fused_computation.111 | custom fusion | flops 512 | bytes 655364 | tf_op jit(solution)/shard_map/scatter-add | solution.py:126
  89.4 4.5 %scatter_custom_fusion.3 = f32[163840]{0:T(1024)} fusion(s32[512]{0:T(512)S(1)} %bitcast.68, f32[512]{0:T(512)S(1)} %reshape.121, f32[]{:T(128)} %constant.17.clone.1), kind=kCustom, calls=%fused_computation.109 | custom fusion | flops 512 | bytes 655364 | tf_op jit(solution)/shard_map/scatter-add | solution.py:132
  93.9 2.4 collective-permute-start.7
  98.1 10.3 %fusion.35 = (f32[40,32,128]{2,1,0:T(8,128)S(1)}, f32[40,32,128]{2,1,0:T(8,128)S(1)}, f32[40,32,128]{2,1,0:T(8,128)S(1)}, f32[40,32,128]{2,1,0:T(8,128)S(1)}) fusion(f32[1,40,32,128]{3,2,1,0:T(8,128)} %param.11, f32[40,32,128]{2,1,0:T(8,128)} %param.15, f32[40,32,128]{2,1,0:T(8,128)S(1)} %copy-done.2, f32[40,32,124]{2,1,0:T(8,128)} %get-tuple-element.112, ...), kind=kLoop, calls=%fused_computation.103 | loop fusion | flops 18677760 | bytes 30564352 | tf_op jit(solution)/shard_map/add | solution.py:142
  108.4 1.3 fusion.66
  109.7 1.3 fusion.67
  112.1 1.3 fusion.69
  114.6 1.3 fusion.71
  117.1 1.4 collective-permute-start.4
  118.5 4.0 %collective-permute-start.5 = (f32[4,32,128]{2,1,0:T(8,128)S(1)}, f32[4,32,128]{2,1,0:T(8,128)S(1)}, u32[]{:S(2)}, u32[]{:S(2)}) collective-permute-start(f32[4,32,128]{2,1,0:T(8,128)S(1)} %get-tuple-element.62), channel_id=1, source_target_pairs={{0,1},{1,2},{2,3},{3,4},{4,5},{5,6},{6,7},{7,8},{8,9},{9,10},{10,1... | collective-permute-start | bytes 196616 | tf_op jit(solution)/shard_map/ppermute | solution.py:18
  122.5 1.3 fusion.74
  123.8 11.9 %fusion.37 = (f32[40,32,128]{2,1,0:T(8,128)}, f32[40,32,128]{2,1,0:T(8,128)S(1)}) fusion(f32[1,40,32,128]{3,2,1,0:T(8,128)} %param.11, f32[40,32,128]{2,1,0:T(8,128)S(1)} %get-tuple-element.10, f32[40,32,128]{2,1,0:T(8,128)S(1)} %copy-done.7, f32[40,32,128]{2,1,0:T(8,128)S(1)} %get-tuple-element.13, f32[40,32,128]{2,1,0:T(8,128)S(1)} %get-tuple-element.12, ...), kind=kLoop, calls=%fused_computation.105 | loop fusion | flops 28016640 | bytes 29384704 | tf_op jit(solution)/shard_map/add | solution.py:152
  135.7 1.4 fusion.49
  137.1 1.3 fusion.50
  139.6 1.2 fusion.52
  142.0 1.3 fusion.54
  144.4 1.3 collective-permute-start.8
  145.7 4.5 %collective-permute-start.9 = (f32[4,32,128]{2,1,0:T(8,128)S(1)}, f32[4,32,128]{2,1,0:T(8,128)S(1)}, u32[]{:S(2)}, u32[]{:S(2)}) collective-permute-start(f32[4,32,128]{2,1,0:T(8,128)S(1)} %get-tuple-element.26), channel_id=1, source_target_pairs={{0,1},{1,2},{2,3},{3,4},{4,5},{5,6},{6,7},{7,8},{8,9},{9,10},{10,1... | collective-permute-start | bytes 196616 | tf_op jit(solution)/shard_map/ppermute | solution.py:18
  151.8 9.0 %add_bitcast_fusion = f32[1,40,32,128]{3,2,1,0:T(8,128)} fusion(f32[40,32,128]{2,1,0:T(8,128)} %param.15, f32[40,32,128]{2,1,0:T(8,128)} %bitcast.63, f32[40,32,128]{2,1,0:T(8,128)} %copy-done.10, f32[40,32,128]{2,1,0:T(8,128)} %copy-done.9, f32[40,32,128]{2,1,0:T(8,128)} %copy-done.8, f32[40,32,128]{2,1,0:T(8,128)S(1)} %copy-done.2, ...), kind=kLoop, calls=%fused_computation.106 | loop fusion | flops 13434880 | bytes 16003072 | tf_op jit(solution)/shard_map/broadcast_in_dim | solution.py:153
  160.8 70.2 %reduce-scatter.2.cloned.1.call-done = f32[40,2,128]{2,0,1:T(8,128)} async-done(((f32[40,32,128]{2,0,1:T(8,128)}), f32[40,2,128]{2,0,1:T(8,128)}) %reduce-scatter.2.cloned.1.call-update) | async-done | bytes 40976 | tf_op jit(solution)/shard_map/reduce_scatter | solution.py:152
  231.1 1.4 copy.58
  (74 shorter events, 19.3 us)
Async XLA Ops:
  7.2 56.7 %copy-start = (f32[1,256,2048]{2,1,0:T(8,128)S(1)}, f32[1,256,2048]{2,1,0:T(8,128)}, u32[]{:S(2)}) copy-start(f32[1,256,2048]{2,1,0:T(8,128)} %param.17) | copy-start | bytes 6291460
  8.9 85.0 %collective-permute-start.3 = (f32[4,32,128]{2,1,0:T(8,128)}, f32[4,32,128]{2,1,0:T(8,128)}, u32[]{:S(2)}, u32[]{:S(2)}) collective-permute-start(f32[4,32,128]{2,1,0:T(8,128)} %get-tuple-element.85), channel_id=1, source_target_pairs={{0,1},{1,2},{2,3},{3,4},{4,5},{5,6},{6,7},{7,8},{8,9},{9,10},{10,1... | collective-permute-start | bytes 196616 | tf_op jit(solution)/shard_map/ppermute | solution.py:18
  13.8 83.4 %collective-permute-start.2 = (f32[4,32,128]{2,1,0:T(8,128)}, f32[4,32,128]{2,1,0:T(8,128)}, u32[]{:S(2)}, u32[]{:S(2)}) collective-permute-start(f32[4,32,128]{2,1,0:T(8,128)} %get-tuple-element.84), channel_id=1, source_target_pairs={{1,0},{2,1},{3,2},{4,3},{5,4},{6,5},{7,6},{8,7},{9,8},{10,9},{11,1... | collective-permute-start | bytes 196616 | tf_op jit(solution)/shard_map/ppermute | solution.py:20
  16.7 81.4 %collective-permute-start = (f32[4,32,128]{2,1,0:T(8,128)}, f32[4,32,128]{2,1,0:T(8,128)}, u32[]{:S(2)}, u32[]{:S(2)}) collective-permute-start(f32[4,32,128]{2,1,0:T(8,128)} %get-tuple-element.101), channel_id=1, source_target_pairs={{1,0},{2,1},{3,2},{4,3},{5,4},{6,5},{7,6},{8,7},{9,8},{10,9},{11,1... | collective-permute-start | bytes 196616 | tf_op jit(solution)/shard_map/ppermute | solution.py:20
  17.9 80.1 %collective-permute-start.1 = (f32[4,32,128]{2,1,0:T(8,128)}, f32[4,32,128]{2,1,0:T(8,128)}, u32[]{:S(2)}, u32[]{:S(2)}) collective-permute-start(f32[4,32,128]{2,1,0:T(8,128)} %get-tuple-element.100), channel_id=1, source_target_pairs={{0,1},{1,2},{2,3},{3,4},{4,5},{5,6},{6,7},{7,8},{8,9},{9,10},{10,1... | collective-permute-start | bytes 196616 | tf_op jit(solution)/shard_map/ppermute | solution.py:18
  27.6 41.3 %all-to-all-start = ((s32[16,1,32]{2,1,0:T(1,128)}), s32[16,1,32]{2,1,0:T(1,128)S(1)}, u32[]{:S(2)}, u32[]{:S(2)}) async-start(s32[16,1,32]{2,1,0:T(1,128)} %all_to_all.9), calls=%async_computation | async-start | bytes 16384 | tf_op jit(solution)/shard_map/all_to_all | solution.py:119
  38.2 85.6 %collective-permute-start.6 = (f32[4,32,128]{2,1,0:T(8,128)}, f32[4,32,128]{2,1,0:T(8,128)}, u32[]{:S(2)}, u32[]{:S(2)}) collective-permute-start(f32[4,32,128]{2,1,0:T(8,128)} %get-tuple-element.44), channel_id=1, source_target_pairs={{1,0},{2,1},{3,2},{4,3},{5,4},{6,5},{7,6},{8,7},{9,8},{10,9},{11,1... | collective-permute-start | bytes 196616 | tf_op jit(solution)/shard_map/ppermute | solution.py:20
  39.5 3.9 %copy-start.2 = (f32[40,32,128]{2,1,0:T(8,128)S(1)}, f32[40,32,128]{2,1,0:T(8,128)}, u32[]{:S(2)}) copy-start(f32[40,32,128]{2,1,0:T(8,128)} %param.16) | copy-start | bytes 1966084
  39.5 3.9 %copy-start.5 = (f32[1,40,32,128]{3,2,1,0:T(8,128)S(1)}, f32[1,40,32,128]{3,2,1,0:T(8,128)}, u32[]{:S(2)}) copy-start(f32[1,40,32,128]{3,2,1,0:T(8,128)} %param.12) | copy-start | bytes 1966084
  53.8 1.6 copy-start.3
  61.5 2.4 copy-start.15
  66.9 31.1 %copy-start.6 = (f32[1,40,32,128]{3,2,1,0:T(8,128)S(1)}, f32[1,40,32,128]{3,2,1,0:T(8,128)}, u32[]{:S(2)}) copy-start(f32[1,40,32,128]{3,2,1,0:T(8,128)} %param.12) | copy-start | bytes 1966084
  68.9 15.8 %all-to-all-start.1 = ((f32[16,32,2]{1,2,0:T(2,128)}), f32[16,32,2]{1,2,0:T(2,128)S(1)}, u32[]{:S(2)}, u32[]{:S(2)}) async-start(f32[16,32,2]{1,2,0:T(2,128)} %copy.56), calls=%async_computation.1 | async-start | bytes 32768 | tf_op jit(solution)/shard_map/all_to_all | solution.py:118
  77.4 153.6 %reduce-scatter.2.cloned.1.call-start = ((), (), s32[]{:S(2)}) async-start(), calls=%async_computation.3 | async-start | bytes 696320 | tf_op jit(solution)/shard_map/reduce_scatter | solution.py:152
  93.9 29.9 %collective-permute-start.7 = (f32[4,32,128]{2,1,0:T(8,128)}, f32[4,32,128]{2,1,0:T(8,128)S(1)}, u32[]{:S(2)}, u32[]{:S(2)}) collective-permute-start(f32[4,32,128]{2,1,0:T(8,128)} %get-tuple-element.45), channel_id=1, source_target_pairs={{0,1},{1,2},{2,3},{3,4},{4,5},{5,6},{6,7},{7,8},{8,9},{9,10},{10,1... | collective-permute-start | bytes 196616 | tf_op jit(solution)/shard_map/ppermute | solution.py:18
  108.4 15.4 %copy-start.8 = (f32[40,32,128]{2,1,0:T(8,128)}, f32[40,32,128]{2,1,0:T(8,128)S(1)}, u32[]{:S(2)}) copy-start(f32[40,32,128]{2,1,0:T(8,128)S(1)} %get-tuple-element.11) | copy-start | bytes 1966084
  108.4 15.4 %copy-start.9 = (f32[40,32,128]{2,1,0:T(8,128)}, f32[40,32,128]{2,1,0:T(8,128)S(1)}, u32[]{:S(2)}) copy-start(f32[40,32,128]{2,1,0:T(8,128)S(1)} %get-tuple-element.12) | copy-start | bytes 1966084
  108.4 15.4 %copy-start.10 = (f32[40,32,128]{2,1,0:T(8,128)}, f32[40,32,128]{2,1,0:T(8,128)S(1)}, u32[]{:S(2)}) copy-start(f32[40,32,128]{2,1,0:T(8,128)S(1)} %get-tuple-element.13) | copy-start | bytes 1966084
  117.0 6.8 %copy-start.7 = (f32[40,32,128]{2,1,0:T(8,128)S(1)}, f32[40,32,128]{2,1,0:T(8,128)}, u32[]{:S(2)}) copy-start(f32[40,32,128]{2,1,0:T(8,128)} %param.15) | copy-start | bytes 1966084
  117.0 6.8 %copy-start.11 = (f32[40,31,128]{2,1,0:T(8,128)S(1)}, f32[40,31,128]{2,1,0:T(8,128)}, u32[]{:S(2)}) copy-start(f32[40,31,128]{2,1,0:T(8,128)} %get-tuple-element.32) | copy-start | bytes 1904644
  117.0 6.8 %copy-start.12 = (f32[40,31,128]{2,1,0:T(8,128)S(1)}, f32[40,31,128]{2,1,0:T(8,128)}, u32[]{:S(2)}) copy-start(f32[40,31,128]{2,1,0:T(8,128)} %get-tuple-element.33) | copy-start | bytes 1904644
  117.0 6.8 %copy-start.13 = (f32[40,32,127]{2,1,0:T(8,128)S(1)}, f32[40,32,127]{2,1,0:T(8,128)}, u32[]{:S(2)}) copy-start(f32[40,32,127]{2,1,0:T(8,128)} %get-tuple-element.34) | copy-start | bytes 1950724
  117.1 6.7 %collective-permute-start.4 = (f32[4,32,128]{2,1,0:T(8,128)S(1)}, f32[4,32,128]{2,1,0:T(8,128)S(1)}, u32[]{:S(2)}, u32[]{:S(2)}) collective-permute-start(f32[4,32,128]{2,1,0:T(8,128)S(1)} %get-tuple-element.63), channel_id=1, source_target_pairs={{1,0},{2,1},{3,2},{4,3},{5,4},{6,5},{7,6},{8,7},{9,8},{10,9},{11,1... | collective-permute-start | bytes 196616 | tf_op jit(solution)/shard_map/ppermute | solution.py:20
  118.5 5.3 %collective-permute-start.5 = (f32[4,32,128]{2,1,0:T(8,128)S(1)}, f32[4,32,128]{2,1,0:T(8,128)S(1)}, u32[]{:S(2)}, u32[]{:S(2)}) collective-permute-start(f32[4,32,128]{2,1,0:T(8,128)S(1)} %get-tuple-element.62), channel_id=1, source_target_pairs={{0,1},{1,2},{2,3},{3,4},{4,5},{5,6},{6,7},{7,8},{8,9},{9,10},{10,1... | collective-permute-start | bytes 196616 | tf_op jit(solution)/shard_map/ppermute | solution.py:18
  135.7 15.8 %copy-start.4 = (f32[40,32,128]{2,1,0:T(8,128)}, f32[40,32,128]{2,1,0:T(8,128)S(1)}, u32[]{:S(2)}) copy-start(f32[40,32,128]{2,1,0:T(8,128)S(1)} %get-tuple-element.9) | copy-start | bytes 1966084
  143.3 7.0 %copy-start.14 = (f32[40,32,128]{2,1,0:T(8,128)S(1)}, f32[40,32,128]{2,1,0:T(8,128)}, u32[]{:S(2)}) copy-start(f32[40,32,128]{2,1,0:T(8,128)} %get-tuple-element.8) | copy-start | bytes 1966084
  144.4 7.4 %collective-permute-start.8 = (f32[4,32,128]{2,1,0:T(8,128)S(1)}, f32[4,32,128]{2,1,0:T(8,128)S(1)}, u32[]{:S(2)}, u32[]{:S(2)}) collective-permute-start(f32[4,32,128]{2,1,0:T(8,128)S(1)} %get-tuple-element.27), channel_id=1, source_target_pairs={{1,0},{2,1},{3,2},{4,3},{5,4},{6,5},{7,6},{8,7},{9,8},{10,9},{11,1... | collective-permute-start | bytes 196616 | tf_op jit(solution)/shard_map/ppermute | solution.py:20
  145.7 6.1 %collective-permute-start.9 = (f32[4,32,128]{2,1,0:T(8,128)S(1)}, f32[4,32,128]{2,1,0:T(8,128)S(1)}, u32[]{:S(2)}, u32[]{:S(2)}) collective-permute-start(f32[4,32,128]{2,1,0:T(8,128)S(1)} %get-tuple-element.26), channel_id=1, source_target_pairs={{0,1},{1,2},{2,3},{3,4},{4,5},{5,6},{6,7},{7,8},{8,9},{9,10},{10,1... | collective-permute-start | bytes 196616 | tf_op jit(solution)/shard_map/ppermute | solution.py:18
  151.8 80.7 %copy-start.1 = (f32[1,256,2048]{2,1,0:T(8,128)S(1)}, f32[1,256,2048]{2,1,0:T(8,128)}, u32[]{:S(2)}) copy-start(f32[1,256,2048]{2,1,0:T(8,128)} %param.17) | copy-start | bytes 6291460
Sparse Core Ops, SparseCore 0:
  151.7 79.3 reduce-scatter.1
where the time goes:
time: 241 us; the launch traced here: 239 us
  waiting for transfers between devices  76.3 us (32%)
  local copies, waits for them, and re-layouts  58.5 us (24%)
  starting transfers between devices  45.2 us (19%)
  other arithmetic  42.1 us (17%)
  between operations  14.4 us (6%)
  matrix products  2.72 us (1%)
    reduce_scatter x1, waiting for transfers between devices, on_device(): lax.psum_scatter(term_first + term_second, 'shot', scatter_dimension=1, t...  70.2 us
    slice x32, local copies, waits for them, and re-layouts, shifted(): portion = lax.slice_in_dim(wavefield, margin, length, axis=dimension)  44.4 us
    ppermute x5, starting transfers between devices, with_halo(): lax.ppermute(tail, axis, [(i, (i + 1) % count) for i in range(ends)])  21.1 us
    add x1, other arithmetic, on_device(): term_first + term_second  11.9 us
    add x1, other arithmetic, on_device(): forward_one = 2.0 * now_field - old_field + stiffness * operate(now_field)  10.3 us
    all_to_all x1, starting transfers between devices, on_device(): lax.all_to_all(cell_buffer, 'slab', split_axis=0, concat_axis=0, tiled=True)  9.04 us
    broadcast_in_dim x1, other arithmetic, on_device(): return (gradient, adjoint_zero[None])  8.98 us
    all_to_all x1, starting transfers between devices, on_device(): lax.all_to_all(value_buffer, 'slab', split_axis=0, concat_axis=0, tiled=T...  8.46 us
  transfers between devices with their start and end apart: 13, of which 2 were waited for; matrix products, arithmetic and copies ran while one was open for 33% of the time, Pallas kernels for 0%

commit v1 on v0

v1 whole, which is shorter than its diff:
```python
import functools

import jax
import jax.numpy as jnp
import ml_dtypes
import numpy as np
from jax import lax
from jax.experimental import pallas as pl
from jax.experimental.pallas import tpu as pltpu
from jax.sharding import PartitionSpec as P

MESH = pl.DeviceIdType.MESH
F32 = jnp.float32
BF16 = jnp.bfloat16

SECOND = (-14350.0, 8064.0, -1008.0, 128.0, -9.0)
FIRST = (0.0, 672.0, -168.0, 32.0, -3.0)
LANES = 128
PAD = 8
HALO = 4
STEP = 4


def along_matrix():
    taps = np.zeros((LANES, 2 * LANES), np.float32)
    for m in range(1, 5):
        for j in range(LANES):
            if j + m < LANES:
                taps[j + m, j] = SECOND[m]
                taps[j + m, LANES + j] = FIRST[m]
            if j - m >= 0:
                taps[j - m, j] = SECOND[m]
                taps[j - m, LANES + j] = -FIRST[m]
    return np.concatenate([taps, taps], axis=0).astype(ml_dtypes.bfloat16)


def two_parts(v):
    high = v.astype(BF16)
    low = (v - high.astype(F32)).astype(BF16)
    return high, low


def three_parts(v):
    high = v.astype(BF16)
    rest = v - high.astype(F32)
    middle = rest.astype(BF16)
    low = (rest - middle.astype(F32)).astype(BF16)
    return high, middle, low


def iota(shape, dim):
    return lax.broadcasted_iota(jnp.int32, shape, dim)


def row_dot(a, b):
    return lax.dot_general(a, b, (((1,), (1,)), ((), ())), preferred_element_type=F32)


def kernel(
    n_shot,
    n_slab,
    planes,
    nx,
    rows,
    samples,
    old_in,
    now_in,
    later_in,
    adj_in,
    stiff_in,
    buoy_in,
    traces_in,
    owner_in,
    plane_in,
    cell_in,
    resample_in,
    along_in,
    grad_out,
    field_out,
    now,
    one,
    adj,
    aone,
    buoy,
    old,
    later,
    stiff,
    traces,
    owner,
    plane,
    cell,
    resample,
    along,
    cb,
    c0,
    c1,
    c2,
    term,
    inj,
    onto,
    part,
    rolled,
    mail,
    gsend,
    grecv,
    gsum,
    result,
    local_sem,
    halo_send,
    halo_recv,
    mail_send,
    mail_recv,
    grad_send,
    grad_recv,
    out_sem,
):
    shot = lax.axis_index("shot")
    slab = lax.axis_index("slab")
    groups = nx // 8
    blocks = planes // STEP
    cap = 2 * rows // n_slab
    per_tile = LANES // cap
    slots = n_slab * cap
    inner = pl.ds(PAD, nx)

    barrier = pltpu.get_barrier_semaphore()

    def greet_slab(k, carry):
        pl.semaphore_signal(
            barrier, inc=1, device_id={"slab": lax.rem(slab + k, n_slab)}, device_id_type=MESH
        )
        return carry

    def greet_shot(k, carry):
        pl.semaphore_signal(
            barrier, inc=1, device_id={"shot": lax.rem(shot + k, n_shot)}, device_id_type=MESH
        )
        return carry

    lax.fori_loop(1, n_slab, greet_slab, 0)
    lax.fori_loop(1, n_shot, greet_shot, 0)

    own = pl.ds(HALO, planes)
    local = [
        (traces_in.at[0], traces),
        (resample_in, resample),
        (owner_in, owner),
        (plane_in, plane),
        (cell_in, cell),
        (along_in, along),
        (buoy_in, buoy.at[own, inner]),
        (stiff_in, stiff),
        (now_in.at[0], now.at[own, inner]),
        (old_in.at[0], old),
        (adj_in.at[0], adj.at[own, inner]),
        (later_in.at[0], later),
    ]
    local = [pltpu.make_async_copy(s, d, local_sem.at[i]) for i, (s, d) in enumerate(local)]
    for copy in local:
        copy.start()

    pl.semaphore_wait(barrier, n_slab - 1 + n_shot - 1)

    top = pl.ds(planes, HALO)
    above = pl.ds(planes + HALO, HALO)
    first = pl.ds(HALO, HALO)
    below = pl.ds(0, HALO)

    def halo(i, low, high, field):
        down = pltpu.make_async_remote_copy(
            src_ref=low,
            dst_ref=field.at[above, inner],
            send_sem=halo_send.at[i, 0],
            recv_sem=halo_recv.at[i, 0],
            device_id={"slab": lax.max(slab - 1, 0)},
            device_id_type=MESH,
        )
        up = pltpu.make_async_remote_copy(
            src_ref=high,
            dst_ref=field.at[below, inner],
            send_sem=halo_send.at[i, 1],
            recv_sem=halo_recv.at[i, 1],
            device_id={"slab": lax.min(slab + 1, n_slab - 1)},
            device_id_type=MESH,
        )
        return down, up

    def halo_start(copies):
        @pl.when(slab > 0)
        def _():
            copies[0].start()

        @pl.when(slab < n_slab - 1)
        def _():
            copies[1].start()

    def halo_arrive(copies):
        @pl.when(slab < n_slab - 1)
        def _():
            copies[0].wait_recv()

        @pl.when(slab > 0)
        def _():
            copies[1].wait_recv()

    def halo_sent(copies):
        @pl.when(slab > 0)
        def _():
            copies[0].wait_send()

        @pl.when(slab < n_slab - 1)
        def _():
            copies[1].wait_send()

    low_in, high_in = pl.ds(0, HALO), pl.ds(planes - HALO, HALO)
    halo_now = halo(0, now_in.at[0, low_in], now_in.at[0, high_in], now)
    halo_buoy = halo(1, buoy_in.at[low_in], buoy_in.at[high_in], buoy)
    halo_adj = halo(2, adj_in.at[0, low_in], adj_in.at[0, high_in], adj)
    halo_one = halo(3, one.at[first, inner], one.at[top, inner], one)
    halo_aone = halo(4, aone.at[first, inner], aone.at[top, inner], aone)
    halo_start(halo_now)
    halo_start(halo_buoy)
    halo_start(halo_adj)

    edge = jnp.zeros((PAD, LANES), F32)

    def clear(z, carry):
        for field in (now, one, adj, aone, buoy):
            field[HALO + z, pl.ds(0, PAD)] = edge
            field[HALO + z, pl.ds(PAD + nx, PAD)] = edge
        return carry

    lax.fori_loop(0, planes, clear, 0)
    outside = jnp.zeros((HALO, nx, LANES), F32)

    @pl.when(slab == 0)
    def _():
        for field in (now, one, adj, aone, buoy):
            field[below, inner] = outside

    @pl.when(slab == n_slab - 1)
    def _():
        for field in (now, one, adj, aone, buoy):
            field[above, inner] = outside

    for copy in local[:5]:
        copy.wait()

    def resampled(i, carry):
        at = pl.ds(pl.multiple_of(i * 32, 32), 32)
        sums = [jnp.zeros((32, LANES), F32)] * 2
        for k in range(samples // LANES):
            lanes = pl.ds(k * LANES, LANES)
            rows_of = traces[at, lanes]
            for j in range(2):
                sums[j] = sums[j] + rows_of * resample[pl.ds(j, 1), lanes]
        for j in range(2):
            part[j, at] = sums[j]
        return carry

    lax.fori_loop(0, rows // 32, resampled, 0)
    ones = jnp.ones((16, LANES), BF16)
    pieces = []
    for j in range(2):
        source = sum(row_dot(ones, piece) for piece in three_parts(part[j]))
        pieces += three_parts(source)

    owners = owner[...]
    member = jnp.where(iota((n_slab, rows), 0) == owners, 1.0, 0.0)
    earlier = jnp.where(iota((rows, rows), 0) < iota((rows, rows), 1), 1.0, 0.0)
    count = jnp.dot(member.astype(BF16), earlier.astype(BF16), preferred_element_type=F32)
    rank = jnp.sum(member * count, axis=0, keepdims=True).astype(jnp.int32)
    target = owners * cap + rank
    place = jnp.where(iota((slots, rows), 0) == target, 1.0, 0.0).astype(BF16)
    cells = cell[...]
    pieces += [
        plane[...].astype(F32),
        (cells // LANES).astype(F32),
        (cells % LANES).astype(F32),
    ]
    table = jnp.zeros((16, rows), F32)
    line = iota((16, rows), 0)
    for i, piece in enumerate(pieces):
        table = jnp.where(line == i, piece.astype(F32), table)
    sorted_rows = row_dot(table.astype(BF16), place)

    def sorted_row(i):
        return sorted_rows[i : i + 1]

    letter = jnp.zeros((8, slots), F32)
    line = iota((8, slots), 0)
    letter_rows = [
        sorted_row(0) + sorted_row(1) + sorted_row(2),
        sorted_row(3) + sorted_row(4) + sorted_row(5),
        sorted_row(6) * float(nx) + sorted_row(7),
        sorted_row(8),
    ]
    for i, letter_row in enumerate(letter_rows):
        letter = jnp.where(line == i, letter_row, letter)
    mine = iota((8, LANES), 1) // cap == lax.rem(slab, per_tile)
    for j in range(per_tile):
        for t in range(slots // LANES):
            tile = letter[:, t * LANES : (t + 1) * LANES]
            if j:
                tile = pltpu.roll(tile, j * cap, 1)
            rolled[j, t] = jnp.where(mine, tile, 0.0)

    def mail_copy(k):
        to = lax.rem(slab + k, n_slab)
        return pltpu.make_async_remote_copy(
            src_ref=rolled.at[lax.rem(n_slab - k, per_tile), to // per_tile],
            dst_ref=mail.at[k],
            send_sem=mail_send.at[k],
            recv_sem=mail_recv.at[k],
            device_id={"slab": to},
            device_id_type=MESH,
        )

    def mail_start(k, carry):
        mail_copy(k).start()
        return carry

    lax.fori_loop(1, n_slab, mail_start, 0)
    mail[0] = rolled[0, slab // per_tile]

    weights = along

    def along_lines(field, at):
        lines = jnp.concatenate([field[at + p, inner] for p in range(STEP)], axis=0)
        return jnp.dot(
            jnp.concatenate(two_parts(lines), axis=1), weights[...], preferred_element_type=F32
        )

    def stencil(field, block, need_second, finish):
        at = HALO + block * STEP
        lines = along_lines(field, at)
        for g in range(groups):
            lo = PAD + 8 * g
            column = [field[at - HALO + q, pl.ds(lo, 8)] for q in range(STEP + 2 * HALO)]
            finished = []
            for p in range(STEP):
                centre = column[HALO + p]
                here = p * nx + 8 * g
                second = None
                if need_second:
                    second = 3.0 * SECOND[0] * centre + lines[here : here + 8, :LANES]
                depth = across = None
                for m in range(1, 5):
                    up, down = column[HALO + p + m], column[HALO + p - m]
                    right = field[at + p, pl.ds(lo + m, 8)]
                    left = field[at + p, pl.ds(lo - m, 8)]
                    if need_second:
                        second = second + SECOND[m] * ((up + down) + (right + left))
                    d, a = FIRST[m] * (up - down), FIRST[m] * (right - left)
                    depth = d if depth is None else depth + d
                    across = a if across is None else across + a
                slopes = (depth, across, lines[here : here + 8, LANES:])
                finished.append(
                    finish(block * STEP + p, pl.ds(8 * g, 8), pl.ds(lo, 8), centre, second, slopes)
                )
            if finished[0] is not None:
                exchange(block, g, finished)

    def waves(field, block, finish):
        def close(z, at, at_padded, centre, second, slopes):
            change = (
                cb[z, at] * second
                + c0[z, at] * slopes[0]
                + c1[z, at] * slopes[1]
                + c2[z, at] * slopes[2]
            )
            return finish(z, at, at_padded, centre, change)

        stencil(field, block, True, close)

    line8 = iota((8, LANES), 0)
    half = line8 < 4
    even = (line8 // 2) % 2 == 0

    def exchange(block, g, v):
        a = [jnp.where(half, v[p], pltpu.roll(v[p + 2], 4, 0)) for p in range(2)]
        b = [jnp.where(half, pltpu.roll(v[p], 4, 0), v[p + 2]) for p in range(2)]
        at = pl.ds(pl.multiple_of(block * 8, 8), 8)
        for i, (c, d) in enumerate((a, b)):
            gsend[4 * g + 2 * i, at] = jnp.where(even, c, pltpu.roll(d, 2, 0))
            gsend[4 * g + 2 * i + 1, at] = jnp.where(even, pltpu.roll(c, 6, 0), d)

    def model_block(block):
        def close(z, at, at_padded, centre, second, slopes):
            k = stiff[z, at]
            cb[z, at] = k * centre * (1.0 / 5040.0)
            k = k * (1.0 / (840.0 * 840.0))
            c0[z, at] = k * slopes[0]
            c1[z, at] = k * slopes[1]
            c2[z, at] = k * slopes[2]

        stencil(buoy, block, False, close)

    def forward_one(block):
        def close(z, at, at_padded, centre, change):
            one[HALO + z, at_padded] = (centre + centre) - old[z, at] + change
            term[z, at] = change

        waves(now, block, close)

    def lines_of(z, at):
        return pl.ds(pl.multiple_of(z * nx + at.start, 8), 8)

    def adjoint_one(block):
        def close(z, at, at_padded, centre, change):
            injected = stiff[z, at] * inj[lines_of(z, at), pl.ds(0, LANES)]
            value = (centre + centre) - later[z, at] + (change + injected)
            aone[HALO + z, at_padded] = value
            term[z, at] = value * term[z, at]

        waves(adj, block, close)

    def gradient(block):
        def close(z, at, at_padded, centre, change):
            return term[z, at] + adj[HALO + z, at_padded] * change

        waves(one, block, close)

    def adjoint_two(block):
        def close(z, at, at_padded, centre, change):
            injected = stiff[z, at] * inj[lines_of(z, at), pl.ds(LANES, LANES)]
            result[z, at] = (
                (centre + centre) - adj[HALO + z, at_padded] + (change + injected)
            )

        waves(aone, block, close)

    def middle(work):
        def body(block, carry):
            work(block)
            return carry

        lax.fori_loop(1, blocks - 1, body, 0)

    def ends(work):
        def body(i, carry):
            work(i * (blocks - 1))
            return carry

        lax.fori_loop(0, 2, body, 0)

    for copy in local[5:10]:
        copy.wait()
    middle(model_block)
    middle(forward_one)
    halo_arrive(halo_buoy)
    halo_arrive(halo_now)
    ends(model_block)
    ends(forward_one)
    halo_start(halo_one)

    def mail_arrive(k, carry):
        mail_copy(k).wait_recv()
        return carry

    lax.fori_loop(1, n_slab, mail_arrive, 0)
    letters = jnp.concatenate(
        [
            sum(mail[q * per_tile + k] for k in range(per_tile))
            for q in range(n_slab // per_tile)
        ],
        axis=1,
    )
    cell_y = letters[3:4].astype(jnp.int32)
    cell_zx = letters[2:3].astype(jnp.int32)
    hit = iota((LANES, slots), 0) == cell_y
    spread = jnp.concatenate(
        [jnp.where(hit, letters[j : j + 1], 0.0) for j in range(2)], axis=0
    ).T
    high, low = two_parts(spread)
    onto[pl.ds(0, slots)] = high
    onto[pl.ds(slots, slots)] = low
    chunk = 4 * nx

    def inject(i, carry):
        base = i * chunk
        pick = jnp.where(iota((chunk, slots), 0) + base == cell_zx, 1.0, 0.0).astype(BF16)
        inj[pl.ds(pl.multiple_of(base, chunk), chunk)] = jnp.dot(
            jnp.concatenate([pick, pick], axis=1), onto[...], preferred_element_type=F32
        )
        return carry

    lax.fori_loop(0, planes * nx // chunk, inject, 0)

    for copy in local[10:]:
        copy.wait()
    halo_arrive(halo_adj)
    ends(adjoint_one)
    halo_start(halo_aone)
    middle(adjoint_one)

    spans = ((8, 8 * (blocks - 2)), (0, 8), (8 * (blocks - 1), 8))

    def grad_copy(c, k):
        to = lax.rem(shot + k, n_shot)
        at = pl.ds(*spans[c])
        return pltpu.make_async_remote_copy(
            src_ref=gsend.at[to, at],
            dst_ref=grecv.at[k, at],
            send_sem=grad_send.at[c, k],
            recv_sem=grad_recv.at[c, k],
            device_id={"shot": to},
            device_id_type=MESH,
        )

    def grad_start(chunks):
        def body(k, carry):
            for c in chunks:
                grad_copy(c, k).start()
            return carry

        lax.fori_loop(1, n_shot, body, 0)

    middle(gradient)
    grad_start((0,))
    halo_arrive(halo_one)
    ends(gradient)
    grad_start((1, 2))

    middle(adjoint_two)
    halo_arrive(halo_aone)
    ends(adjoint_two)
    field_copy = pltpu.make_async_copy(result, field_out, out_sem.at[0])
    field_copy.start()

    def grad_arrive(k, carry):
        for c in range(3):
            grad_copy(c, k).wait_recv()
        return carry

    lax.fori_loop(1, n_shot, grad_arrive, 0)
    gsum[...] = gsend[shot] + sum(grecv[k] for k in range(1, n_shot))
    grad_write = pltpu.make_async_copy(gsum, grad_out, out_sem.at[1])
    grad_write.start()

    for copies in (halo_now, halo_buoy, halo_adj, halo_one, halo_aone):
        halo_sent(copies)

    def mail_sent(k, carry):
        mail_copy(k).wait_send()
        return carry

    lax.fori_loop(1, n_slab, mail_sent, 0)

    def grad_sent(k, carry):
        for c in range(3):
            grad_copy(c, k).wait_send()
        return carry

    lax.fori_loop(1, n_shot, grad_sent, 0)
    field_copy.wait()
    grad_write.wait()


def on_device(
    pressure_old,
    pressure_now,
    adjoint_later,
    adjoint_now,
    stiffness,
    buoyancy,
    traces,
    owner_slab,
    depth_plane,
    station_cell,
    resampler,
):
    n_shot, n_slab = lax.axis_size("shot"), lax.axis_size("slab")
    planes, nx, _ = buoyancy.shape
    rows, samples = traces.shape[1:]
    slots = 2 * rows
    own_rows = planes * (nx // n_shot)
    padded = pltpu.VMEM((planes + 2 * HALO, nx + 2 * PAD, LANES), F32)
    plain = pltpu.VMEM((planes, nx, LANES), F32)
    dma = pltpu.SemaphoreType.DMA
    grad, field = pl.pallas_call(
        functools.partial(kernel, n_shot, n_slab, planes, nx, rows, samples),
        name="imaging",
        out_shape=(
            jax.ShapeDtypeStruct((own_rows, LANES), F32),
            jax.ShapeDtypeStruct((planes, nx, LANES), F32),
        ),
        in_specs=[pl.BlockSpec(memory_space=pl.ANY)] * 12,
        out_specs=(pl.BlockSpec(memory_space=pl.ANY),) * 2,
        scratch_shapes=[
            padded,
            padded,
            padded,
            padded,
            padded,
            plain,
            plain,
            plain,
            pltpu.VMEM((rows, samples), F32),
            pltpu.VMEM((1, rows), jnp.int32),
            pltpu.VMEM((1, rows), jnp.int32),
            pltpu.VMEM((1, rows), jnp.int32),
            pltpu.VMEM((2, samples), F32),
            pltpu.VMEM((2 * LANES, 2 * LANES), BF16),
            plain,
            plain,
            plain,
            plain,
            plain,
            pltpu.VMEM((planes * nx, 2 * LANES), F32),
            pltpu.VMEM((2 * slots, 2 * LANES), BF16),
            pltpu.VMEM((2, rows, LANES), F32),
            pltpu.VMEM((LANES * n_slab // slots, slots // LANES, 8, LANES), F32),
            pltpu.VMEM((n_slab, 8, LANES), F32),
            pltpu.VMEM((n_shot, own_rows, LANES), F32),
            pltpu.VMEM((n_shot, own_rows, LANES), F32),
            pltpu.VMEM((own_rows, LANES), F32),
            plain,
            dma((12,)),
            dma((5, 2)),
            dma((5, 2)),
            dma((n_slab,)),
            dma((n_slab,)),
            dma((3, n_shot)),
            dma((3, n_shot)),
            dma((2,)),
        ],
        compiler_params=pltpu.CompilerParams(
            collective_id=0, has_side_effects=True, vmem_limit_bytes=56 * 1024 * 1024
        ),
    )(
        pressure_old,
        pressure_now,
        adjoint_later,
        adjoint_now,
        stiffness,
        buoyancy,
        traces,
        owner_slab.reshape(1, rows),
        depth_plane,
        station_cell,
        resampler,
        jnp.asarray(along_matrix()),
    )
    return grad.reshape(planes, nx // n_shot, LANES), field[None]


def solution(mesh):
    return jax.shard_map(
        on_device,
        mesh=mesh,
        in_specs=(
            P("shot", "slab", None, None),
            P("shot", "slab", None, None),
            P("shot", "slab", None, None),
            P("shot", "slab", None, None),
            P("slab", None, None),
            P("slab", None, None),
            P("shot", "slab", None),
            P("shot", "slab", None),
            P("shot", "slab"),
            P("shot", "slab"),
            P(),
        ),
        out_specs=(P("slab", "shot", None), P("shot", "slab", None, None)),
        check_vma=False,
    )
```

time: 241 us -> 42.8 us (0.18)
  waiting for transfers between devices: 76.3 us -> 0 us
  local copies, waits for them, and re-layouts: 58.5 us -> 3.37 us
  starting transfers between devices: 45.2 us -> 0 us
  other arithmetic: 42.1 us -> 0 us
  Pallas kernels: 0 us -> 38.6 us
  between operations: 14.4 us -> 0.64 us
  matrix products: 2.72 us -> 0 us
    reduce_scatter x1 -> x0, waiting for transfers between devices: 70.2 us -> none  [on_device(): lax.psum_scatter(term_first + term_second, 'shot', scatter_dimension=1, t...]
    slice x38 -> x0, local copies, waits for them, and re-layouts: 49.2 us -> none  [the longest x32 44.4 us: shifted(): portion = lax.slice_in_dim(wavefield, margin, length, axis=dimension)]
    pallas_call x0 -> x1, Pallas kernels: none -> 38.6 us  [on_device(): pl.pallas_call(functools.partial(kernel, n_shot, n_slab, planes, nx, rows...]
    ppermute x10 -> x0, starting transfers between devices: 27.7 us -> none  [the longest x5 21.1 us: with_halo(): lax.ppermute(tail, axis, [(i, (i + 1) % count) for i in range(ends)])]
    add x3 -> x0, other arithmetic: 22.9 us -> none  [the longest x1 11.9 us: on_device(): term_first + term_second]
    all_to_all x2 -> x0, starting transfers between devices: 17.5 us -> none  [the longest x1 9.04 us: on_device(): lax.all_to_all(cell_buffer, 'slab', split_axis=0, concat_axis=0, tiled=True)]
    broadcast_in_dim x1 -> x0, other arithmetic: 8.98 us -> none  [on_device(): return (gradient, adjoint_zero[None])]
    scatter-add x2 -> x0, other arithmetic: 8.91 us -> none  [the longest x1 4.46 us: on_device(): inject_second = jnp.zeros((volume,), jnp.float32).at[flat_cells].add(arri...]
  transfers between devices with their start and end apart: 13 -> 0, of which waited for: 2 -> 0; matrix products, arithmetic and copies ran while one was open for 33% -> 0% of each run, Pallas kernels for 0% -> 0%
where the time goes in v1:
time: 42.8 us; the launch traced here: 42.6 us
  Pallas kernels  38.6 us (90%)
  local copies, waits for them, and re-layouts  3.37 us (8%)
  between operations  0.64 us (1%)
    pallas_call x1, Pallas kernels, on_device(): pl.pallas_call(functools.partial(kernel, n_shot, n_slab, planes, nx, rows...  38.6 us
    unnamed x2, local copies, waits for them, and re-layouts  3.37 us

profile of v1, /device:TPU:1, one launch (start us, length us, event | category | flops | bytes accessed | tf_op | source)
XLA Modules:
  0.0 42.6 jit_solution(10468612795991885724)
XLA Ops:
  0.6 38.6 %imaging.1 = (f32[80,128]{1,0:T(8,128)}, f32[40,32,128]{2,1,0:T(8,128)}) custom-call(f32[1,40,32,128]{3,2,1,0:T(8,128)} %old_in.1, f32[1,40,32,128]{3,2,1,0:T(8,128)} %now_in.1, f32[1,40,32,128]{3,2,1,0:T(8,128)} %later_in.1, f32[1,40,32,128]{3,2,1,0:T(8,128)} %adj_in.1, f32[40,32,128]{2,1,0:T(8,128)} %stiff_in.1, f32[40,32,128]{2,1,0:T(8,128)} %buoy_in.1, ...), custom_call_target="tpu_custom_call" | custom-call | tf_op jit(solution)/shard_map/imaging/pallas_call | solution.py:581
  39.2 1.4 %copy.16 = f32[40,2,128]{2,1,0:T(2,128)} copy(f32[40,2,128]{2,1,0:T(2,128)} %bitcast.4) | data formatting | bytes 81920
  40.6 2.0 %copy.17 = f32[1,40,32,128]{3,2,1,0:T(8,128)} copy(f32[1,40,32,128]{3,2,1,0:T(8,128)} %bitcast.3) | data formatting | bytes 1310720

commit v2 on v1

--- a/solution.py
+++ b/solution.py
@@ -103,8 +103,10 @@
     mail,
     gsend,
     grecv,
-    gsum,
-    result,
+    lines_a,
+    lines_b,
+    lines_c,
+    lines_d,
     local_sem,
     halo_send,
     halo_recv,
@@ -112,7 +114,6 @@
     mail_recv,
     grad_send,
     grad_recv,
-    out_sem,
 ):
     shot = lax.axis_index("shot")
     slab = lax.axis_index("slab")
@@ -122,44 +123,46 @@
     per_tile = LANES // cap
     slots = n_slab * cap
     inner = pl.ds(PAD, nx)
+    even_lines, odd_lines = (lines_a, lines_b), (lines_c, lines_d)
 
     barrier = pltpu.get_barrier_semaphore()
-
-    def greet_slab(k, carry):
-        pl.semaphore_signal(
-            barrier, inc=1, device_id={"slab": lax.rem(slab + k, n_slab)}, device_id_type=MESH
-        )
-        return carry
-
-    def greet_shot(k, carry):
-        pl.semaphore_signal(
-            barrier, inc=1, device_id={"shot": lax.rem(shot + k, n_shot)}, device_id_type=MESH
-        )
-        return carry
-
-    lax.fori_loop(1, n_slab, greet_slab, 0)
-    lax.fori_loop(1, n_shot, greet_shot, 0)
 
     own = pl.ds(HALO, planes)
     local = [
+        (buoy_in, buoy.at[own, inner]),
+        (stiff_in, stiff),
+        (along_in, along),
         (traces_in.at[0], traces),
         (resample_in, resample),
         (owner_in, owner),
         (plane_in, plane),
         (cell_in, cell),
-        (along_in, along),
-        (buoy_in, buoy.at[own, inner]),
-        (stiff_in, stiff),
         (now_in.at[0], now.at[own, inner]),
         (old_in.at[0], old),
         (adj_in.at[0], adj.at[own, inner]),
         (later_in.at[0], later),
     ]
     local = [pltpu.make_async_copy(s, d, local_sem.at[i]) for i, (s, d) in enumerate(local)]
-    for copy in local:
+    for copy in local[:3]:
         copy.start()
 
-    pl.semaphore_wait(barrier, n_slab - 1 + n_shot - 1)
+    def greet_slab(k, carry):
+        pl.semaphore_signal(
+            barrier, inc=1, device_id={"slab": lax.rem(slab + k, n_slab)}, device_id_type=MESH
+        )
+        return carry
+
+    def greet_shot(k, carry):
+        pl.semaphore_signal(
+            barrier, inc=1, device_id={"shot": lax.rem(shot + k, n_shot)}, device_id_type=MESH
+        )
+        return carry
+
+    lax.fori_loop(1, n_slab, greet_slab, 0)
+    lax.fori_loop(1, n_shot, greet_shot, 0)
+
+    for copy in local[3:]:
+        copy.start()
 
     top = pl.ds(planes, HALO)
     above = pl.ds(planes + HALO, HALO)
@@ -218,10 +221,6 @@
     halo_adj = halo(2, adj_in.at[0, low_in], adj_in.at[0, high_in], adj)
     halo_one = halo(3, one.at[first, inner], one.at[top, inner], one)
     halo_aone = halo(4, aone.at[first, inner], aone.at[top, inner], aone)
-    halo_start(halo_now)
-    halo_start(halo_buoy)
-    halo_start(halo_adj)
-
     edge = jnp.zeros((PAD, LANES), F32)
 
     def clear(z, carry):
@@ -243,97 +242,15 @@
         for field in (now, one, adj, aone, buoy):
             field[above, inner] = outside
 
-    for copy in local[:5]:
-        copy.wait()
-
-    def resampled(i, carry):
-        at = pl.ds(pl.multiple_of(i * 32, 32), 32)
-        sums = [jnp.zeros((32, LANES), F32)] * 2
-        for k in range(samples // LANES):
-            lanes = pl.ds(k * LANES, LANES)
-            rows_of = traces[at, lanes]
-            for j in range(2):
-                sums[j] = sums[j] + rows_of * resample[pl.ds(j, 1), lanes]
-        for j in range(2):
-            part[j, at] = sums[j]
-        return carry
-
-    lax.fori_loop(0, rows // 32, resampled, 0)
-    ones = jnp.ones((16, LANES), BF16)
-    pieces = []
-    for j in range(2):
-        source = sum(row_dot(ones, piece) for piece in three_parts(part[j]))
-        pieces += three_parts(source)
-
-    owners = owner[...]
-    member = jnp.where(iota((n_slab, rows), 0) == owners, 1.0, 0.0)
-    earlier = jnp.where(iota((rows, rows), 0) < iota((rows, rows), 1), 1.0, 0.0)
-    count = jnp.dot(member.astype(BF16), earlier.astype(BF16), preferred_element_type=F32)
-    rank = jnp.sum(member * count, axis=0, keepdims=True).astype(jnp.int32)
-    target = owners * cap + rank
-    place = jnp.where(iota((slots, rows), 0) == target, 1.0, 0.0).astype(BF16)
-    cells = cell[...]
-    pieces += [
-        plane[...].astype(F32),
-        (cells // LANES).astype(F32),
-        (cells % LANES).astype(F32),
-    ]
-    table = jnp.zeros((16, rows), F32)
-    line = iota((16, rows), 0)
-    for i, piece in enumerate(pieces):
-        table = jnp.where(line == i, piece.astype(F32), table)
-    sorted_rows = row_dot(table.astype(BF16), place)
-
-    def sorted_row(i):
-        return sorted_rows[i : i + 1]
-
-    letter = jnp.zeros((8, slots), F32)
-    line = iota((8, slots), 0)
-    letter_rows = [
-        sorted_row(0) + sorted_row(1) + sorted_row(2),
-        sorted_row(3) + sorted_row(4) + sorted_row(5),
-        sorted_row(6) * float(nx) + sorted_row(7),
-        sorted_row(8),
-    ]
-    for i, letter_row in enumerate(letter_rows):
-        letter = jnp.where(line == i, letter_row, letter)
-    mine = iota((8, LANES), 1) // cap == lax.rem(slab, per_tile)
-    for j in range(per_tile):
-        for t in range(slots // LANES):
-            tile = letter[:, t * LANES : (t + 1) * LANES]
-            if j:
-                tile = pltpu.roll(tile, j * cap, 1)
-            rolled[j, t] = jnp.where(mine, tile, 0.0)
-
-    def mail_copy(k):
-        to = lax.rem(slab + k, n_slab)
-        return pltpu.make_async_remote_copy(
-            src_ref=rolled.at[lax.rem(n_slab - k, per_tile), to // per_tile],
-            dst_ref=mail.at[k],
-            send_sem=mail_send.at[k],
-            recv_sem=mail_recv.at[k],
-            device_id={"slab": to},
-            device_id_type=MESH,
+    def fill(field, block, lines):
+        at = HALO + block * STEP
+        whole = jnp.concatenate([field[at + p, inner] for p in range(STEP)], axis=0)
+        lines[...] = jnp.dot(
+            jnp.concatenate(two_parts(whole), axis=1), along[...], preferred_element_type=F32
         )
 
-    def mail_start(k, carry):
-        mail_copy(k).start()
-        return carry
-
-    lax.fori_loop(1, n_slab, mail_start, 0)
-    mail[0] = rolled[0, slab // per_tile]
-
-    weights = along
-
-    def along_lines(field, at):
-        lines = jnp.concatenate([field[at + p, inner] for p in range(STEP)], axis=0)
-        return jnp.dot(
-            jnp.concatenate(two_parts(lines), axis=1), weights[...], preferred_element_type=F32
-        )
-
-    def stencil(field, block, need_second, finish):
+    def stencil(field, block, lines, need_second, finish):
         at = HALO + block * STEP
-        lines = along_lines(field, at)
         for g in range(groups):
             lo = PAD + 8 * g
             column = [field[at - HALO + q, pl.ds(lo, 8)] for q in range(STEP + 2 * HALO)]
@@ -361,7 +278,7 @@
             if finished[0] is not None:
                 exchange(block, g, finished)
 
-    def waves(field, block, finish):
+    def waves(field, block, lines, finish):
         def close(z, at, at_padded, centre, second, slopes):
             change = (
                 cb[z, at] * second
@@ -371,7 +288,7 @@
             )
             return finish(z, at, at_padded, centre, change)
 
-        stencil(field, block, True, close)
+        stencil(field, block, lines, True, close)
 
     line8 = iota((8, LANES), 0)
     half = line8 < 4
@@ -385,7 +302,7 @@
             gsend[4 * g + 2 * i, at] = jnp.where(even, c, pltpu.roll(d, 2, 0))
             gsend[4 * g + 2 * i + 1, at] = jnp.where(even, pltpu.roll(c, 6, 0), d)
 
-    def model_block(block):
+    def model_block(block, lines):
         def close(z, at, at_padded, centre, second, slopes):
             k = stiff[z, at]
             cb[z, at] = k * centre * (1.0 / 5040.0)
@@ -394,64 +311,164 @@
             c1[z, at] = k * slopes[1]
             c2[z, at] = k * slopes[2]
 
-        stencil(buoy, block, False, close)
-
-    def forward_one(block):
+        stencil(buoy, block, lines, False, close)
+
+    def forward_one(block, lines):
         def close(z, at, at_padded, centre, change):
             one[HALO + z, at_padded] = (centre + centre) - old[z, at] + change
             term[z, at] = change
 
-        waves(now, block, close)
+        waves(now, block, lines, close)
 
     def lines_of(z, at):
         return pl.ds(pl.multiple_of(z * nx + at.start, 8), 8)
 
-    def adjoint_one(block):
+    def adjoint_one(block, lines):
         def close(z, at, at_padded, centre, change):
             injected = stiff[z, at] * inj[lines_of(z, at), pl.ds(0, LANES)]
             value = (centre + centre) - later[z, at] + (change + injected)
             aone[HALO + z, at_padded] = value
             term[z, at] = value * term[z, at]
 
-        waves(adj, block, close)
-
-    def gradient(block):
+        waves(adj, block, lines, close)
+
+    def gradient(block, lines):
         def close(z, at, at_padded, centre, change):
             return term[z, at] + adj[HALO + z, at_padded] * change
 
-        waves(one, block, close)
-
-    def adjoint_two(block):
+        waves(one, block, lines, close)
+
+    def adjoint_two(block, lines):
         def close(z, at, at_padded, centre, change):
             injected = stiff[z, at] * inj[lines_of(z, at), pl.ds(LANES, LANES)]
-            result[z, at] = (
+            field_out[z, at] = (
                 (centre + centre) - adj[HALO + z, at_padded] + (change + injected)
             )
 
-        waves(aone, block, close)
-
-    def middle(work):
-        def body(block, carry):
-            work(block)
+        waves(aone, block, lines, close)
+
+    def middle(works, begin, end, fresh=True):
+        if fresh:
+            for j, (field, work) in enumerate(works):
+                fill(field, 1 + 2 * begin, even_lines[j])
+
+        def body(i, carry):
+            block = 1 + 2 * i
+            for j, (field, work) in enumerate(works):
+                fill(field, block + 1, odd_lines[j])
+            for j, (field, work) in enumerate(works):
+                work(block, even_lines[j])
+            for j, (field, work) in enumerate(works):
+                fill(field, block + 2, even_lines[j])
+            for j, (field, work) in enumerate(works):
+                work(block + 1, odd_lines[j])
             return carry
 
-        lax.fori_loop(1, blocks - 1, body, 0)
-
-    def ends(work):
-        def body(i, carry):
-            work(i * (blocks - 1))
-            return carry
-
-        lax.fori_loop(0, 2, body, 0)
-
-    for copy in local[5:10]:
+        lax.fori_loop(begin, end, body, 0)
+
+    def ends(field, work):
+        fill(field, 0, even_lines[0])
+        fill(field, blocks - 1, odd_lines[0])
+        work(0, even_lines[0])
+        work(blocks - 1, odd_lines[0])
+
+    pairs = (blocks - 2) // 2
+    for copy in local[:3]:
         copy.wait()
-    middle(model_block)
-    middle(forward_one)
+    middle(((buoy, model_block),), 0, pairs)
+
+    pl.semaphore_wait(barrier, n_slab - 1 + n_shot - 1)
+    halo_start(halo_now)
+    halo_start(halo_buoy)
+    halo_start(halo_adj)
+
+    for copy in local[3:8]:
+        copy.wait()
+
+    def resampled(i, carry):
+        at = pl.ds(pl.multiple_of(i * 32, 32), 32)
+        sums = [jnp.zeros((32, LANES), F32)] * 2
+        for k in range(samples // LANES):
+            lanes = pl.ds(k * LANES, LANES)
+            rows_of = traces[at, lanes]
+            for j in range(2):
+                sums[j] = sums[j] + rows_of * resample[pl.ds(j, 1), lanes]
+        for j in range(2):
+            part[j, at] = sums[j]
+        return carry
+
+    lax.fori_loop(0, rows // 32, resampled, 0)
+    ones = jnp.ones((16, LANES), BF16)
+    pieces = []
+    for j in range(2):
+        source = sum(row_dot(ones, piece) for piece in three_parts(part[j]))
+        pieces += three_parts(source)
+
+    owners = owner[...]
+    member = jnp.where(iota((n_slab, rows), 0) == owners, 1.0, 0.0)
+    earlier = jnp.where(iota((rows, rows), 0) < iota((rows, rows), 1), 1.0, 0.0)
+    count = jnp.dot(member.astype(BF16), earlier.astype(BF16), preferred_element_type=F32)
+    rank = jnp.sum(member * count, axis=0, keepdims=True).astype(jnp.int32)
+    target = owners * cap + rank
+    place = jnp.where(iota((slots, rows), 0) == target, 1.0, 0.0).astype(BF16)
+    cells = cell[...]
+    pieces += [
+        plane[...].astype(F32),
+        (cells // LANES).astype(F32),
+        (cells % LANES).astype(F32),
+    ]
+    table = jnp.zeros((16, rows), F32)
+    line = iota((16, rows), 0)
+    for i, piece in enumerate(pieces):
+        table = jnp.where(line == i, piece.astype(F32), table)
+    sorted_rows = row_dot(table.astype(BF16), place)
+
+    def sorted_row(i):
+        return sorted_rows[i : i + 1]
+
+    letter = jnp.zeros((8, slots), F32)
+    line = iota((8, slots), 0)
+    letter_rows = [
+        sorted_row(0) + sorted_row(1) + sorted_row(2),
+        sorted_row(3) + sorted_row(4) + sorted_row(5),
+        sorted_row(6) * float(nx) + sorted_row(7),
+        sorted_row(8),
+    ]
+    for i, letter_row in enumerate(letter_rows):
+        letter = jnp.where(line == i, letter_row, letter)
+    mine = iota((8, LANES), 1) // cap == lax.rem(slab, per_tile)
+    for j in range(per_tile):
+        for t in range(slots // LANES):
+            tile = letter[:, t * LANES : (t + 1) * LANES]
+            if j:
+                tile = pltpu.roll(tile, j * cap, 1)
+            rolled[j, t] = jnp.where(mine, tile, 0.0)
+
+    def mail_copy(k):
+        to = lax.rem(slab + k, n_slab)
+        return pltpu.make_async_remote_copy(
+            src_ref=rolled.at[lax.rem(n_slab - k, per_tile), to // per_tile],
+            dst_ref=mail.at[k],
+            send_sem=mail_send.at[k],
+            recv_sem=mail_recv.at[k],
+            device_id={"slab": to},
+            device_id_type=MESH,
+        )
+
+    def mail_start(k, carry):
+        mail_copy(k).start()
+        return carry
+
+    lax.fori_loop(1, n_slab, mail_start, 0)
+    mail[0] = rolled[0, slab // per_tile]
+
+    for copy in local[8:10]:
+        copy.wait()
+    middle(((now, forward_one),), 0, pairs)
     halo_arrive(halo_buoy)
     halo_arrive(halo_now)
-    ends(model_block)
-    ends(forward_one)
+    ends(buoy, model_block)
+    ends(now, forward_one)
     halo_start(halo_one)
 
     def mail_arrive(k, carry):
@@ -475,7 +492,7 @@
     high, low = two_parts(spread)
     onto[pl.ds(0, slots)] = high
     onto[pl.ds(slots, slots)] = low
-    chunk = 4 * nx
+    chunk = planes * nx // 4
 
     def inject(i, carry):
         base = i * chunk
@@ -485,16 +502,17 @@
         )
         return carry
 
-    lax.fori_loop(0, planes * nx // chunk, inject, 0)
+    lax.fori_loop(0, 4, inject, 0)
 
     for copy in local[10:]:
         copy.wait()
     halo_arrive(halo_adj)
-    ends(adjoint_one)
+    ends(adj, adjoint_one)
     halo_start(halo_aone)
-    middle(adjoint_one)
-
-    spans = ((8, 8 * (blocks - 2)), (0, 8), (8 * (blocks - 1), 8))
+
+    parts = (0, pairs // 2, pairs)
+    spans = [(8 + 16 * lo, 16 * (hi - lo)) for lo, hi in zip(parts, parts[1:])]
+    spans += [(0, 8), (8 * (blocks - 1), 8)]
 
     def grad_copy(c, k):
         to = lax.rem(shot + k, n_shot)
@@ -516,27 +534,25 @@
 
         lax.fori_loop(1, n_shot, body, 0)
 
-    middle(gradient)
-    grad_start((0,))
+    both = ((adj, adjoint_one), (one, gradient))
+    for c in range(2):
+        middle(both, parts[c], parts[c + 1], fresh=c == 0)
+        grad_start((c,))
     halo_arrive(halo_one)
-    ends(gradient)
-    grad_start((1, 2))
-
-    middle(adjoint_two)
+    ends(one, gradient)
+    grad_start((2, 3))
+
+    middle(((aone, adjoint_two),), 0, pairs)
     halo_arrive(halo_aone)
-    ends(adjoint_two)
-    field_copy = pltpu.make_async_copy(result, field_out, out_sem.at[0])
-    field_copy.start()
+    ends(aone, adjoint_two)
 
     def grad_arrive(k, carry):
-        for c in range(3):
+        for c in range(len(spans)):
             grad_copy(c, k).wait_recv()
         return carry
 
     lax.fori_loop(1, n_shot, grad_arrive, 0)
-    gsum[...] = gsend[shot] + sum(grecv[k] for k in range(1, n_shot))
-    grad_write = pltpu.make_async_copy(gsum, grad_out, out_sem.at[1])
-    grad_write.start()
+    grad_out[...] = gsend[shot] + sum(grecv[k] for k in range(1, n_shot))
 
     for copies in (halo_now, halo_buoy, halo_adj, halo_one, halo_aone):
         halo_sent(copies)
@@ -548,13 +564,20 @@
     lax.fori_loop(1, n_slab, mail_sent, 0)
 
     def grad_sent(k, carry):
-        for c in range(3):
+        for c in range(len(spans)):
             grad_copy(c, k).wait_send()
         return carry
 
     lax.fori_loop(1, n_shot, grad_sent, 0)
+
+
+def hand_on(grad_in, field_in, grad_out, field_out, sem):
+    grad_copy = pltpu.make_async_copy(grad_in, grad_out, sem.at[0])
+    field_copy = pltpu.make_async_copy(field_in, field_out, sem.at[1])
+    grad_copy.start()
+    field_copy.start()
+    grad_copy.wait()
     field_copy.wait()
-    grad_write.wait()
 
 
 def on_device(
@@ -582,11 +605,11 @@
         functools.partial(kernel, n_shot, n_slab, planes, nx, rows, samples),
         name="imaging",
         out_shape=(
-            jax.ShapeDtypeStruct((own_rows, LANES), F32),
-            jax.ShapeDtypeStruct((planes, nx, LANES), F32),
+            pltpu.VMEM((own_rows, LANES), F32),
+            pltpu.VMEM((planes, nx, LANES), F32),
         ),
-        in_specs=[pl.BlockSpec(memory_space=pl.ANY)] * 12,
-        out_specs=(pl.BlockSpec(memory_space=pl.ANY),) * 2,
+        in_specs=[pl.BlockSpec(memory_space=pltpu.HBM)] * 12,
+        out_specs=(pl.BlockSpec(memory_space=pltpu.VMEM),) * 2,
         scratch_shapes=[
             padded,
             padded,
@@ -614,19 +637,17 @@
             pltpu.VMEM((n_slab, 8, LANES), F32),
             pltpu.VMEM((n_shot, own_rows, LANES), F32),
             pltpu.VMEM((n_shot, own_rows, LANES), F32),
-            pltpu.VMEM((own_rows, LANES), F32),
-            plain,
+            *[pltpu.VMEM((STEP * nx, 2 * LANES), F32)] * 4,
             dma((12,)),
             dma((5, 2)),
             dma((5, 2)),
             dma((n_slab,)),
             dma((n_slab,)),
-            dma((3, n_shot)),
-            dma((3, n_shot)),
-            dma((2,)),
+            dma((4, n_shot)),
+            dma((4, n_shot)),
         ],
         compiler_params=pltpu.CompilerParams(
-            collective_id=0, has_side_effects=True, vmem_limit_bytes=56 * 1024 * 1024
+            collective_id=0, has_side_effects=True, vmem_limit_bytes=61 * 1024 * 1024
         ),
     )(
         pressure_old,
@@ -642,6 +663,18 @@
         resampler,
         jnp.asarray(along_matrix()),
     )
+    grad, field = pl.pallas_call(
+        hand_on,
+        name="hand_on",
+        out_shape=(
+            jax.ShapeDtypeStruct((own_rows, LANES), F32),
+            jax.ShapeDtypeStruct((planes, nx, LANES), F32),
+        ),
+        in_specs=[pl.BlockSpec(memory_space=pl.ANY)] * 2,
+        out_specs=(pl.BlockSpec(memory_space=pltpu.HBM),) * 2,
+        scratch_shapes=[dma((2,))],
+        compiler_params=pltpu.CompilerParams(vmem_limit_bytes=1024 * 1024),
+    )(grad, field)
     return grad.reshape(planes, nx // n_shot, LANES), field[None]
 
 

time: 42.8 us -> 37.9 us (0.89)
  local copies, waits for them, and re-layouts: 3.37 us -> 0 us
  Pallas kernels: 38.6 us -> 37.2 us
    unnamed x2 -> x0, local copies, waits for them, and re-layouts: 3.37 us -> none
    pallas_call x1, Pallas kernels: 38.6 us -> 36.3 us  [on_device(): pl.pallas_call(functools.partial(kernel, n_shot, n_slab, planes, nx, rows...]
    pallas_call x0 -> x1, Pallas kernels: none -> 0.87 us  [on_device(): pl.pallas_call(hand_on, name='hand_on', out_shape=(jax.ShapeDtypeStruct((...]
where the time goes in v2:
time: 37.9 us
  Pallas kernels  37.2 us (98%)
  between operations  0.64 us (2%)
    pallas_call x1, Pallas kernels, on_device(): pl.pallas_call(functools.partial(kernel, n_shot, n_slab, planes, nx, rows...  36.3 us
    pallas_call x1, Pallas kernels, on_device(): pl.pallas_call(hand_on, name='hand_on', out_shape=(jax.ShapeDtypeStruct((...  0.87 us

profile of v2, /device:TPU:1, one launch (start us, length us, event | category | flops | bytes accessed | tf_op | source)
XLA Modules:
  0.0 37.9 jit_solution(1374012462733781289)
XLA Ops:
  0.6 36.3 %imaging.1 = (f32[80,128]{1,0:T(8,128)S(1)}, f32[40,32,128]{2,1,0:T(8,128)S(1)}) custom-call(f32[1,40,32,128]{3,2,1,0:T(8,128)} %old_in.1, f32[1,40,32,128]{3,2,1,0:T(8,128)} %now_in.1, f32[1,40,32,128]{3,2,1,0:T(8,128)} %later_in.1, f32[1,40,32,128]{3,2,1,0:T(8,128)} %adj_in.1, f32[40,32,128]{2,1,0:T(8,128)} %stiff_in.1, f32[40,32,128]{2,1,0:T(8,128)} %buoy_in.1, ...), custom_call_target="tpu_custom_call" | custom-call | tf_op jit(solution)/shard_map/imaging/pallas_call | solution.py:604
  37.0 0.9 %hand_on.1 = (f32[80,128]{1,0:T(8,128)}, f32[40,32,128]{2,1,0:T(8,128)}) custom-call(f32[80,128]{1,0:T(8,128)S(1)} %get-tuple-element.6.grad_in, f32[40,32,128]{2,1,0:T(8,128)S(1)} %get-tuple-element.7.field_in), custom_call_target="tpu_custom_call" | custom-call | tf_op jit(solution)/shard_map/hand_on/pallas_call | solution.py:666
